TPU v7x, 32 devices: a whole 2x2x4 slice. The times are simulated.
32 devices in a mesh: dp: 8 (over z, x), mp: 4 (over y, core).
Axes of the slice: x: 2, y: 2, z: 4, core: 2. Of those that a mesh axis runs over, the one named last changes fastest.
Arguments:
- tokens: bfloat16 [12288, 768], P(('dp', 'mp')), may hold values from -6 to 6
- out_grad: bfloat16 [12288, 768], P(('dp', 'mp')), may hold values from -6 to 6
- segment_ids: int32 [24, 512], P('dp'), may hold values from 0 to 1, as said below
- group_ids: int32 [24, 512], P('dp'), may hold values from 0 to 3
- answer_ids: int32 [24, 512], P('dp'), may hold values 0 or 1
- pad_lengths: int32 [24], P('dp'), may hold values from 256 to 512, as said below
- qkv_master: float32 [3, 768, 768], P(None, 'dp', 'mp'), may hold values from -0.21875 to 0.21875
- out_master: float32 [768, 768], P('mp', 'dp'), may hold values from -1.25 to 1.25
- up_master: float32 [768, 3072], P('dp', 'mp')
- down_master: float32 [3072, 768], P('mp', 'dp'), may hold values from -0.15625 to 0.15625
- norm_master: float32 [6, 4, 192], P(None, 'mp', 'dp')
- bias_master: float32 [4, 1152], P('mp', 'dp'), may hold values from -2 to 2
- qkv_first: float32 [3, 768, 768], P(None, 'dp', 'mp')
- out_first: float32 [768, 768], P('mp', 'dp')
- up_first: float32 [768, 3072], P('dp', 'mp')
- down_first: float32 [3072, 768], P('mp', 'dp')
- norm_first: float32 [6, 4, 192], P(None, 'mp', 'dp')
- bias_first: float32 [4, 1152], P('mp', 'dp')
- qkv_second: float32 [3, 768, 768], P(None, 'dp', 'mp')
- out_second: float32 [768, 768], P('mp', 'dp')
- up_second: float32 [768, 3072], P('dp', 'mp')
- down_second: float32 [3072, 768], P('mp', 'dp')
- norm_second: float32 [6, 4, 192], P(None, 'mp', 'dp')
- bias_second: float32 [4, 1152], P('mp', 'dp')
Outputs:
- block_out: bfloat16 [12288, 768], P(('dp', 'mp'))
- input_grad: bfloat16 [12288, 768], P(('dp', 'mp'))
- grad_norm: float32 [], replicated
- new_qkv: float32 [3, 768, 768], P(None, 'dp', 'mp')
- new_out: float32 [768, 768], P('mp', 'dp')
- new_up: float32 [768, 3072], P('dp', 'mp')
- new_down: float32 [3072, 768], P('mp', 'dp')
- new_norm: float32 [6, 4, 192], P(None, 'mp', 'dp')
- new_bias: float32 [4, 1152], P('mp', 'dp')
- first_qkv: float32 [3, 768, 768], P(None, 'dp', 'mp')
- first_out: float32 [768, 768], P('mp', 'dp')
- first_up: float32 [768, 3072], P('dp', 'mp')
- first_down: float32 [3072, 768], P('mp', 'dp')
- first_norm: float32 [6, 4, 192], P(None, 'mp', 'dp')
- first_bias: float32 [4, 1152], P('mp', 'dp')
- second_qkv: float32 [3, 768, 768], P(None, 'dp', 'mp')
- second_out: float32 [768, 768], P('mp', 'dp')
- second_up: float32 [768, 3072], P('dp', 'mp')
- second_down: float32 [3072, 768], P('mp', 'dp')
- second_norm: float32 [6, 4, 192], P(None, 'mp', 'dp')
- second_bias: float32 [4, 1152], P('mp', 'dp')
Inputs may be any that keep to these rules, and one draw needn't show every extreme that they name: `segment_ids`: each sequence's question (segment 0) is a first run of 1 to 129 positions; segment 1 follows. `pad_lengths`: some sequence in every draw has no padding.
All inputs are finite; a program needn't handle non-finite values. No bound on the sum of `answer_ids` on one device may be relied on, other than what follows from the above.
Results may differ from a plain program's by a relative error of at most 0.025.
Values may be sent and summed in bfloat16 or wider, within the bound.
A program may use at most 128 MiB of HBM per device.

v0:
```python
import jax
import jax.numpy as jnp
from jax import lax
from jax.sharding import PartitionSpec as P

HD = 64
STEP = 5


norm_epsilon = 1e-06
adam_epsilon = 1e-08
learn_rates = (0.02, 0.1, 0.02, 0.02, 0.5, 0.5)
beta_first = 0.5
beta_second = 0.5
decay_rate = 0.01
clip_limit = 0.05
mask_fill = -1000000000.0
score_scale = 0.125


def layer_norm(rows, gain, shift):
    mean = jnp.mean(rows, -1, keepdims=True)
    centred = rows - mean
    spread = jnp.mean(centred * centred, -1, keepdims=True)
    return centred * lax.rsqrt(spread + norm_epsilon) * gain + shift


def gelu_exact(values):
    return jax.nn.gelu(values, approximate=False)


def visible_mask(segment, group, answer, length):
    positions = jnp.arange(segment.shape[-1], dtype=jnp.int32)
    valid_key = positions[None, :] < length[:, None]
    open_key = (segment == 0) | (answer == 1)
    rule = (
        (segment[:, :, None] == 0) | open_key[:, None, :] | (group[:, :, None] == group[:, None, :])
    )
    return rule & valid_key[:, None, :]


def masked_scores(queries, keys, allowed):
    scores = (
        jnp.einsum("qhe,khe->hqk", queries, keys, preferred_element_type=jnp.float32) * score_scale
    )
    return jnp.where(allowed[None], scores, mask_fill)


def attend(items):
    queries, keys, values, allowed = items
    scores = masked_scores(queries, keys, allowed)
    peak = jnp.max(scores, -1, keepdims=True)
    log_total = peak + jnp.log(jnp.sum(jnp.exp(scores - peak), -1, keepdims=True))
    shares = jnp.exp(scores - log_total).astype(jnp.bfloat16)
    mixed = jnp.einsum("hqk,khe->qhe", shares, values, preferred_element_type=jnp.float32)
    return (mixed.astype(jnp.bfloat16), log_total)


def attend_back(items):
    queries, keys, values, allowed, log_total, grad_mixed = items
    scores = masked_scores(queries, keys, allowed)
    shares = jnp.exp(scores - log_total)
    shares_low = shares.astype(jnp.bfloat16)
    grad_shares = jnp.einsum("qhe,khe->hqk", grad_mixed, values, preferred_element_type=jnp.float32)
    grad_values = jnp.einsum(
        "hqk,qhe->khe", shares_low, grad_mixed, preferred_element_type=jnp.float32
    )
    centre = jnp.sum(shares * grad_shares, -1, keepdims=True)
    grad_scores = (shares * (grad_shares - centre)).astype(jnp.bfloat16)
    grad_queries = (
        jnp.einsum("hqk,khe->qhe", grad_scores, keys, preferred_element_type=jnp.float32)
        * score_scale
    )
    grad_keys = (
        jnp.einsum("hqk,qhe->khe", grad_scores, queries, preferred_element_type=jnp.float32)
        * score_scale
    )
    return jnp.stack([grad_queries, grad_keys, grad_values], 1).astype(jnp.bfloat16)


def adam_update(weight, grad, first, second, factor, decayed, rate):
    clipped = grad * factor
    first_new = beta_first * first + (1.0 - beta_first) * clipped
    second_new = beta_second * second + (1.0 - beta_second) * clipped * clipped
    ratio = (
        first_new
        / (1.0 - beta_first**STEP)
        / (jnp.sqrt(second_new / (1.0 - beta_second**STEP)) + adam_epsilon)
    )
    if decayed:
        ratio = ratio + decay_rate * weight
    return (weight - rate * ratio, first_new, second_new)


def body(
    tokens,
    out_grad,
    segment_ids,
    group_ids,
    answer_ids,
    pad_lengths,
    qkv_master,
    out_master,
    up_master,
    down_master,
    norm_master,
    bias_master,
    qkv_first,
    out_first,
    up_first,
    down_first,
    norm_first,
    bias_first,
    qkv_second,
    out_second,
    up_second,
    down_second,
    norm_second,
    bias_second,
):
    masters = (qkv_master, out_master, up_master, down_master, norm_master, bias_master)
    firsts = (qkv_first, out_first, up_first, down_first, norm_first, bias_first)
    seconds = (qkv_second, out_second, up_second, down_second, norm_second, bias_second)
    owner_dims = (1, 1, 0, 1, 2, 1)
    lowered = [weight.astype(jnp.bfloat16) for weight in masters]
    joint_weight, out_weight, up_weight, down_weight, table_part, column_part = (
        lax.all_gather(lowered[0], "dp", axis=1, tiled=True),
        lax.all_gather(lowered[1], "dp", axis=1, tiled=True),
        lax.all_gather(lowered[2], "dp", axis=0, tiled=True),
        lax.all_gather(lowered[3], "dp", axis=1, tiled=True),
        lax.all_gather(lowered[4], "dp", axis=2, tiled=True),
        lax.all_gather(lowered[5], "dp", axis=1, tiled=True),
    )
    rows_full, gain_table = (
        lax.all_gather(tokens, "mp", axis=0, tiled=True),
        lax.all_gather(table_part, "mp", axis=1, tiled=True),
    )
    model_width = rows_full.shape[1]
    gains = gain_table.reshape(6, model_width).astype(jnp.float32)
    local_width = joint_weight.shape[2]
    heads_here = local_width // HD
    column_bias = column_part[0].astype(jnp.float32)
    bias_query = column_bias[:local_width]
    bias_value = column_bias[local_width : 2 * local_width]
    bias_up = column_bias[2 * local_width :]
    bias_joint = jnp.stack([bias_query, jnp.zeros_like(bias_query), bias_value])
    seqs_here = segment_ids.shape[0]
    length = segment_ids.shape[1]
    visible = visible_mask(segment_ids, group_ids, answer_ids, pad_lengths)
    projected = jnp.einsum(
        "td,cdj->tcj", rows_full, joint_weight, preferred_element_type=jnp.float32
    )
    projected = (projected + bias_joint[None]).astype(jnp.bfloat16)
    shaped = projected.reshape(seqs_here, length, 3, heads_here, HD)
    queries = shaped[:, :, 0]
    keys = shaped[:, :, 1]
    values = shaped[:, :, 2]
    mixed, log_total = lax.map(attend, (queries, keys, values, visible))
    mixed_flat = mixed.reshape(seqs_here * length, local_width)
    branch_part = jnp.dot(mixed_flat, out_weight, preferred_element_type=jnp.float32)
    branch = lax.psum_scatter(
        branch_part.astype(jnp.bfloat16), "mp", scatter_dimension=0, tiled=True
    ).astype(jnp.float32)
    first_sum = tokens.astype(jnp.float32) + (branch + gains[2])
    normed, norm_one_back = jax.vjp(layer_norm, first_sum, gains[0], gains[1])
    normed_full = lax.all_gather(normed.astype(jnp.bfloat16), "mp", axis=0, tiled=True)
    hidden = jnp.dot(normed_full, up_weight, preferred_element_type=jnp.float32) + bias_up
    active, gelu_back = jax.vjp(gelu_exact, hidden)
    active_low = active.astype(jnp.bfloat16)
    second_part = jnp.dot(active_low, down_weight, preferred_element_type=jnp.float32)
    second = lax.psum_scatter(
        second_part.astype(jnp.bfloat16), "mp", scatter_dimension=0, tiled=True
    ).astype(jnp.float32)
    result, norm_two_back = jax.vjp(layer_norm, normed + (second + gains[5]), gains[3], gains[4])
    grad_sum_two, grad_gain_two, grad_shift_two = norm_two_back(out_grad.astype(jnp.float32))
    grad_second = grad_sum_two.astype(jnp.bfloat16)
    grad_bias_down = jnp.sum(grad_second.astype(jnp.float32), 0)
    second_full = lax.all_gather(grad_second, "mp", axis=0, tiled=True)
    grad_down = jnp.einsum("tf,td->fd", active_low, second_full, preferred_element_type=jnp.float32)
    grad_active = jnp.einsum(
        "td,fd->tf", second_full, down_weight, preferred_element_type=jnp.float32
    )
    grad_hidden = gelu_back(grad_active)[0].astype(jnp.bfloat16)
    grad_bias_up = jnp.sum(grad_hidden.astype(jnp.float32), 0)
    grad_up = jnp.einsum("td,tf->df", normed_full, grad_hidden, preferred_element_type=jnp.float32)
    normed_part = jnp.einsum(
        "tf,df->td", grad_hidden, up_weight, preferred_element_type=jnp.float32
    )
    normed_back = lax.psum_scatter(
        normed_part.astype(jnp.bfloat16), "mp", scatter_dimension=0, tiled=True
    ).astype(jnp.float32)
    grad_sum_one, grad_gain_one, grad_shift_one = norm_one_back(grad_sum_two + normed_back)
    grad_branch = grad_sum_one.astype(jnp.bfloat16)
    grad_bias_out = jnp.sum(grad_branch.astype(jnp.float32), 0)
    branch_full = lax.all_gather(grad_branch, "mp", axis=0, tiled=True)
    grad_out = jnp.einsum("tj,td->jd", mixed_flat, branch_full, preferred_element_type=jnp.float32)
    grad_mixed = jnp.einsum(
        "td,jd->tj", branch_full, out_weight, preferred_element_type=jnp.float32
    )
    grad_mixed = grad_mixed.astype(jnp.bfloat16).reshape(seqs_here, length, heads_here, HD)
    grad_joint = lax.map(attend_back, (queries, keys, values, visible, log_total, grad_mixed))
    grad_joint = grad_joint.reshape(seqs_here * length, 3, local_width)
    grad_bias_query = jnp.sum(grad_joint[:, 0].astype(jnp.float32), 0)
    grad_bias_value = jnp.sum(grad_joint[:, 2].astype(jnp.float32), 0)
    grad_qkv = jnp.einsum("td,tcj->cdj", rows_full, grad_joint, preferred_element_type=jnp.float32)
    input_part = jnp.einsum(
        "tcj,cdj->td", grad_joint, joint_weight, preferred_element_type=jnp.float32
    )
    table_grad = jnp.stack(
        [
            grad_gain_one,
            grad_shift_one,
            grad_bias_out,
            grad_gain_two,
            grad_shift_two,
            grad_bias_down,
        ]
    )
    table_grad = table_grad.reshape(6, lax.axis_size("mp"), local_width)
    input_back, table_sum = (
        lax.psum_scatter(
            input_part.astype(jnp.bfloat16), "mp", scatter_dimension=0, tiled=True
        ).astype(jnp.float32),
        lax.psum_scatter(
            table_grad.astype(jnp.bfloat16), "mp", scatter_dimension=1, tiled=True
        ).astype(jnp.float32),
    )
    input_grad = (grad_sum_one + input_back).astype(jnp.bfloat16)
    column_grad = jnp.concatenate([grad_bias_query, grad_bias_value, grad_bias_up])[None]
    summed = lax.psum((grad_qkv, grad_out, grad_up, grad_down, table_sum, column_grad), "dp")
    place = lax.axis_index("dp")
    owned = [
        lax.dynamic_slice_in_dim(
            total, place * master.shape[dimension], master.shape[dimension], dimension
        )
        for total, master, dimension in zip(summed, masters, owner_dims)
    ]
    squares = jnp.zeros((), jnp.float32)
    for grad in owned:
        squares = squares + jnp.sum(grad * grad)
    total_squares = lax.psum(squares, ("dp", "mp"))
    grad_norm = jnp.sqrt(total_squares)
    factor = jnp.minimum(1.0, clip_limit / grad_norm)
    updated = []
    for index in range(6):
        updated.append(
            adam_update(
                masters[index],
                owned[index],
                firsts[index],
                seconds[index],
                factor,
                index < 4,
                learn_rates[index],
            )
        )
    return (
        result.astype(jnp.bfloat16),
        input_grad,
        grad_norm,
        updated[0][0],
        updated[1][0],
        updated[2][0],
        updated[3][0],
        updated[4][0],
        updated[5][0],
        updated[0][1],
        updated[1][1],
        updated[2][1],
        updated[3][1],
        updated[4][1],
        updated[5][1],
        updated[0][2],
        updated[1][2],
        updated[2][2],
        updated[3][2],
        updated[4][2],
        updated[5][2],
    )


def solution(mesh):
    in_specs = (
        P(("dp", "mp"), None),
        P(("dp", "mp"), None),
        P("dp", None),
        P("dp", None),
        P("dp", None),
        P("dp"),
        P(None, "dp", "mp"),
        P("mp", "dp"),
        P("dp", "mp"),
        P("mp", "dp"),
        P(None, "mp", "dp"),
        P("mp", "dp"),
        P(None, "dp", "mp"),
        P("mp", "dp"),
        P("dp", "mp"),
        P("mp", "dp"),
        P(None, "mp", "dp"),
        P("mp", "dp"),
        P(None, "dp", "mp"),
        P("mp", "dp"),
        P("dp", "mp"),
        P("mp", "dp"),
        P(None, "mp", "dp"),
        P("mp", "dp"),
    )
    out_specs = (
        P(("dp", "mp"), None),
        P(("dp", "mp"), None),
        P(),
        P(None, "dp", "mp"),
        P("mp", "dp"),
        P("dp", "mp"),
        P("mp", "dp"),
        P(None, "mp", "dp"),
        P("mp", "dp"),
        P(None, "dp", "mp"),
        P("mp", "dp"),
        P("dp", "mp"),
        P("mp", "dp"),
        P(None, "mp", "dp"),
        P("mp", "dp"),
        P(None, "dp", "mp"),
        P("mp", "dp"),
        P("dp", "mp"),
        P("mp", "dp"),
        P(None, "mp", "dp"),
        P("mp", "dp"),
    )
    return jax.shard_map(body, mesh=mesh, in_specs=in_specs, out_specs=out_specs, check_vma=False)
```

profile of v0, /device:TPU:0, one launch (start us, length us, event | category | flops | bytes accessed | tf_op | source)
XLA Modules:
  0.0 764.3 jit_solution(15605650422538360400)
XLA Ops:
  11.7 23.1 %all-reduce = bf16[1152]{0:T(1024)(128)(2,1)S(1)} all-reduce(bf16[1152]{0:T(1024)(128)(2,1)S(1)} %dynamic-update-slice), channel_id=1, replica_groups=mesh['dp'=8,'mp'=4] {'dp'}, use_global_device_ids=true, to_apply=%add | all-reduce | flops 1152 | bytes 4608
  36.0 35.4 %all_gather.34 = bf16[3,768,192]{2,0,1:T(4,128)(2,1)S(1)} all-gather(bf16[3,96,192]{2,0,1:T(4,128)(2,1)S(1)} %copy.120), channel_id=1, replica_groups=mesh['dp'=8,'mp'=4] {'dp'}, dimensions={1}, use_global_device_ids=true | all-gather | bytes 995328 | tf_op jit(solution)/shard_map/all_gather | solution.py:127
  72.5 31.0 %all_gather.36 = bf16[192,768]{0,1:T(8,128)(2,1)S(1)} all-gather(bf16[192,96]{0,1:T(8,128)(2,1)S(1)} %copy.126), channel_id=1, replica_groups=mesh['dp'=8,'mp'=4] {'dp'}, dimensions={1}, use_global_device_ids=true | all-gather | bytes 331776 | tf_op jit(solution)/shard_map/all_gather | solution.py:128
  109.5 5.2 reshape.254
  117.5 9.3 %while.22 = (s32[]{:T(128)}, bf16[3,512,3,64]{1,3,2,0:T(8,128)(2,1)S(1)}, f32[3,3,512,1]{2,1,3,0:T(4,128)}, bf16[3,512,3,64]{1,3,2,0:T(8,128)(2,1)S(1)}, pred[3,...) while((s32[]{:T(128)}, ...), condition=%wide.region_3.4_spmd, body=%wide.region_0.3_spmd.sunk | while | flops 210074112 | bytes 11590233 | solution.py:158
  131.7 30.6 %all_gather.37 = bf16[6,1,192]{0,1,2:T(2,128)(2,1)S(1)} all-gather(bf16[6,1,24]{0,1,2:T(2,128)(2,1)S(1)} %copy.128), channel_id=1, replica_groups=mesh['dp'=8,'mp'=4] {'dp'}, dimensions={2}, use_global_device_ids=true | all-gather | bytes 2592 | tf_op jit(solution)/shard_map/all_gather | solution.py:131
  162.4 5.2 all_gather.38
  175.2 24.5 %all-gather.9.cloned.1.call-done = bf16[1536,768]{1,0:T(8,128)(2,1)} async-done(((bf16[384,768]{1,0:T(8,128)(2,1)}), bf16[1536,768]{1,0:T(8,128)(2,1)}) %all-gather.9.cloned.1.call-update) | async-done | bytes 2359312 | tf_op jit(solution)/shard_map/all_gather | solution.py:166
  199.7 15.2 %multiply_convert_fusion.1 = (bf16[1536,768]{1,0:T(8,128)(2,1)}, f32[1536,768]{1,0:T(8,128)}, f32[1536,768]{1,0:T(8,128)}) fusion(f32[768]{0:T(1024)S(1)} %slice_reduce_fusion.6, bf16[1536,768]{1,0:T(8,128)(2,1)} %all-gather.9.cloned.1.call-done, bf16[768,768]{1,0:T(8,128)(2,1)} %all-gather.11.cloned.1.call-done), kind=kOutput, calls=%fused_computation.64 | convolution fusion | flops 1889796096 | bytes 15338496 | tf_op jit(solution)/shard_map/dot_general | solution.py:167
  215.0 29.2 %all-gather.13.cloned.1.call-done = bf16[768,768]{0,1:T(8,128)(2,1)} async-done(((bf16[768,96]{0,1:T(8,128)(2,1)}), bf16[768,768]{0,1:T(8,128)(2,1)}) %all-gather.13.cloned.1.call-update) | async-done | bytes 1179664 | tf_op jit(solution)/shard_map/all_gather | solution.py:130
  244.2 5.4 convolution_convert_fusion.1
  250.5 30.7 %reduce-scatter.8.cloned.1.call-done = bf16[384,768]{1,0:T(8,128)(2,1)} async-done(((bf16[1536,768]{1,0:T(8,128)(2,1)}), bf16[384,768]{1,0:T(8,128)(2,1)}) %reduce-scatter.8.cloned.1.call-update) | async-done | bytes 589840 | tf_op jit(solution)/shard_map/reduce_scatter | solution.py:171
  288.8 24.0 %all-gather.15.cloned.1.call-done = bf16[1536,768]{1,0:T(8,128)(2,1)} async-done(((bf16[384,768]{1,0:T(8,128)(2,1)}), bf16[1536,768]{1,0:T(8,128)(2,1)}) %all-gather.15.cloned.1.call-update) | async-done | bytes 2359312 | tf_op jit(solution)/shard_map/all_gather | solution.py:178
  312.8 8.8 %convert_reduce_fusion = (f32[768]{0:T(1024)}, bf16[1536,768]{1,0:T(8,128)(2,1)S(1)}) fusion(f32[1536,768]{1,0:T(8,128)} %get-tuple-element.323, f32[1536,768]{1,0:T(8,128)} %get-tuple-element.336, f32[768]{0:T(1024)} %copy-done.50, bf16[1536,768]{1,0:T(8,128)(2,1)} %all-gather.15.cloned.1.call-done, bf16[768,768]{0,1:T(8,128)(2,1)} %all-gather.13.cloned.1.call-done), kind=kOutput, calls=%fused_computation.62 | convolution fusion | flops 1831992576 | bytes 15341568 | tf_op jit(solution)/shard_map/td,fd->tf/dot_general | solution.py:180
  326.5 33.2 %reduce-scatter.10.cloned.1.call-done = bf16[384,768]{1,0:T(8,128)(2,1)} async-done(((bf16[1536,768]{1,0:T(8,128)(2,1)}), bf16[384,768]{1,0:T(8,128)(2,1)}) %reduce-scatter.10.cloned.1.call-update) | async-done | bytes 589840 | tf_op jit(solution)/shard_map/reduce_scatter | solution.py:189
  366.8 6.0 fusion.92
  377.6 12.8 %all-gather.17.cloned.1.call-done = bf16[1536,768]{1,0:T(8,128)(2,1)} async-done(((bf16[384,768]{1,0:T(8,128)(2,1)}), bf16[1536,768]{1,0:T(8,128)(2,1)}) %all-gather.17.cloned.1.call-update) | async-done | bytes 2359312 | tf_op jit(solution)/shard_map/all_gather | solution.py:195
  393.6 23.1 %while.23 = (s32[]{:T(128)}, bf16[3,512,3,3,64]{1,4,3,2,0:T(8,128)(2,1)}, bf16[3,512,3,64]{1,3,2,0:T(8,128)(2,1)S(1)}, pred[3,512,512]{1,2,0:T(8,128)(4,1)}, bf1...) while((s32[]{:T(128)}, ...), condition=%wide.region_17.18_spmd, body=%wide.region_15.17_spmd.sunk | while | flops 512653824 | bytes 27560560 | solution.py:201
  419.7 3.8 reshape.257
  423.4 5.1 fusion.57
  440.5 39.3 %all-reduce.1 = (f32[6,1,192]{2,0,1:T(8,128)S(1)}, f32[1,1152]{1,0:T(1,128)S(1)}) all-reduce(bf16[6,1,192]{2,0,1:T(8,128)(2,1)} %reduce-scatter.14.cloned.1.call-done, f32[1,1152]{1,0:T(1,128)S(1)} %broadcast_in_dim.81), channel_id=1, replica_groups=mesh['dp'=8,'mp'=4] {'dp'}, use_global_device_ids=true, to_apply=%region_34.35 | all-reduce | flops 2304 | bytes 16128 | tf_op jit(solution)/shard_map/psum | solution.py:230
  481.1 184.4 %all-reduce.5.cloned.1.call-done = (f32[3,768,192]{1,2,0:T(8,128)}, f32[192,768]{1,0:T(8,128)}, f32[768,768]{1,0:T(8,128)}, f32[768,768]{0,1:T(8,128)}) async-done(((f32[3,768,192]{1,2,0:T(8,128)}, f32[192,768]{1,0:T(8,128)}, f32[768,768]{1,0:T(8,128)}, f32[768,768]{0,1:T(8,128)}), (f32[3,768,192]{1,2,0:T(8,128)}, f32[192,768]{1,0:T(8,128)}, f32[768,768]{1,0:T(8,128)}, ...) | async-done | bytes 7077904 | tf_op jit(solution)/shard_map/psum | solution.py:230
  676.2 24.0 %reduce-scatter.12.cloned.1.call-done = bf16[384,768]{1,0:T(8,128)(2,1)} async-done(((bf16[1536,768]{1,0:T(8,128)(2,1)}), bf16[384,768]{1,0:T(8,128)(2,1)}) %reduce-scatter.12.cloned.1.call-update) | async-done | bytes 589840 | tf_op jit(solution)/shard_map/reduce_scatter | solution.py:221
  702.4 39.3 %psum.55 = f32[]{:T(128)} all-reduce(f32[]{:T(128)S(6)} %add.276), channel_id=1, replica_groups=mesh['dp'=8,'mp'=4] {'dp','mp'}, use_global_device_ids=true, to_apply=%region_41.42 | all-reduce | flops 1 | bytes 8 | tf_op jit(solution)/shard_map/psum | solution.py:241
  (283 shorter events, 125.0 us)
Async XLA Ops:
  8.0 96.8 %all-gather.7.cloned.1.call-start = ((), (), s32[]{:S(2)}) async-start(), calls=%async_computation.5 | async-start | bytes 2949120 | tf_op jit(solution)/shard_map/all_gather | solution.py:135
  8.8 159.1 %reduce-scatter.6.cloned.1.call-start = ((), (), s32[]{:S(2)}) async-start(), calls=%async_computation.6 | async-start | bytes 2949120 | tf_op jit(solution)/shard_map/reduce_scatter | solution.py:161
  34.8 68.7 %copy-start.38 = (f32[1,1152]{1,0:T(1,128)}, f32[1,1152]{1,0:T(1,128)S(1)}, u32[]{:S(2)}) copy-start(f32[1,1152]{1,0:T(1,128)S(1)} %reshape.261) | copy-start | bytes 13828
  35.9 67.5 %copy-start.54 = (s32[3]{0:T(128)S(1)}, s32[3]{0:T(128)}, u32[]{:S(2)}) copy-start(s32[3]{0:T(128)} %param.33) | copy-start | bytes 40
  36.0 67.7 %copy-start.46 = (s32[3,512]{1,0:T(4,128)S(1)}, s32[3,512]{1,0:T(4,128)}, u32[]{:S(2)}) copy-start(s32[3,512]{1,0:T(4,128)} %param.32) | copy-start | bytes 18436
  36.0 67.7 %copy-start.47 = (s32[3,512]{1,0:T(4,128)S(1)}, s32[3,512]{1,0:T(4,128)}, u32[]{:S(2)}) copy-start(s32[3,512]{1,0:T(4,128)} %param.30) | copy-start | bytes 18436
  36.0 67.7 %copy-start.37 = (s32[3,512]{1,0:T(4,128)S(1)}, s32[3,512]{1,0:T(4,128)}, u32[]{:S(2)}) copy-start(s32[3,512]{1,0:T(4,128)} %param.31) | copy-start | bytes 18436
  130.7 44.5 %all-gather.11.cloned.1.call-start = ((), (), s32[]{:S(2)}) async-start(), calls=%async_computation.8 | async-start | bytes 1327104 | tf_op jit(solution)/shard_map/all_gather | solution.py:129
  131.5 68.2 %all-gather.9.cloned.1.call-start = ((), (), s32[]{:S(2)}) async-start(), calls=%async_computation.7 | async-start | bytes 2949120 | tf_op jit(solution)/shard_map/all_gather | solution.py:166
  172.0 72.2 %all-gather.13.cloned.1.call-start = ((), (), s32[]{:S(2)}) async-start(), calls=%async_computation.9 | async-start | bytes 1327104 | tf_op jit(solution)/shard_map/all_gather | solution.py:130
  172.7 108.5 %reduce-scatter.8.cloned.1.call-start = ((), (), s32[]{:S(2)}) async-start(), calls=%async_computation.10 | async-start | bytes 2949120 | tf_op jit(solution)/shard_map/reduce_scatter | solution.py:171
  249.6 63.1 %all-gather.15.cloned.1.call-start = ((), (), s32[]{:S(2)}) async-start(), calls=%async_computation.11 | async-start | bytes 2949120 | tf_op jit(solution)/shard_map/all_gather | solution.py:178
  288.6 71.1 %reduce-scatter.10.cloned.1.call-start = ((), (), s32[]{:S(2)}) async-start(), calls=%async_computation.12 | async-start | bytes 2949120 | tf_op jit(solution)/shard_map/reduce_scatter | solution.py:189
  326.5 63.9 %all-gather.17.cloned.1.call-start = ((), (), s32[]{:S(2)}) async-start(), calls=%async_computation.13 | async-start | bytes 2949120 | tf_op jit(solution)/shard_map/all_gather | solution.py:195
  366.4 74.1 %reduce-scatter.14.cloned.1.call-start = ((), (), s32[]{:S(2)}) async-start(), calls=%async_computation.15 | async-start | bytes 20480 | tf_op jit(solution)/shard_map/reduce_scatter | solution.py:224
  377.3 288.2 %all-reduce.5.cloned.1.call-start = ((), (), s32[]{:S(2)}) async-start(), calls=%async_computation.16 | async-start | bytes 14155776 | tf_op jit(solution)/shard_map/psum | solution.py:230
  430.0 270.2 %reduce-scatter.12.cloned.1.call-start = ((), (), s32[]{:S(2)}) async-start(), calls=%async_computation.14 | async-start | bytes 2949120 | tf_op jit(solution)/shard_map/reduce_scatter | solution.py:221
  436.2 264.1 %copy-start.4 = (f32[384,768]{1,0:T(8,128)S(1)}, f32[384,768]{1,0:T(8,128)}, u32[]{:S(2)}) copy-start(f32[384,768]{1,0:T(8,128)} %copy-done.3) | copy-start | bytes 3538948
  439.4 303.1 %copy-start.43 = (f32[6,1,24]{2,1,0:T(1,128)S(1)}, f32[6,1,24]{2,1,0:T(1,128)}, u32[]{:S(2)}) copy-start(f32[6,1,24]{2,1,0:T(1,128)} %param.38) | copy-start | bytes 1732
  439.6 305.4 %copy-start.23 = (f32[3,96,192]{1,2,0:T(8,128)S(1)}, f32[3,96,192]{1,2,0:T(8,128)}, u32[]{:S(2)}) copy-start(f32[3,96,192]{1,2,0:T(8,128)} %copy.137) | copy-start | bytes 663556
  702.3 46.7 %copy-start.53 = (f32[1,144]{1,0:T(1,128)S(1)}, f32[1,144]{1,0:T(1,128)}, u32[]{:S(2)}) copy-start(f32[1,144]{1,0:T(1,128)} %param.51) | copy-start | bytes 1732
  702.3 47.4 %copy-start.20 = (f32[768,96]{0,1:T(8,128)S(1)}, f32[768,96]{0,1:T(8,128)}, u32[]{:S(2)}) copy-start(f32[768,96]{0,1:T(8,128)} %param.37) | copy-start | bytes 884740
  702.3 47.4 %copy-start.29 = (f32[768,96]{0,1:T(8,128)S(1)}, f32[768,96]{0,1:T(8,128)}, u32[]{:S(2)}) copy-start(f32[768,96]{0,1:T(8,128)} %param.43) | copy-start | bytes 884740
  702.4 47.4 %copy-start.30 = (f32[768,96]{0,1:T(8,128)S(1)}, f32[768,96]{0,1:T(8,128)}, u32[]{:S(2)}) copy-start(f32[768,96]{0,1:T(8,128)} %param.49) | copy-start | bytes 884740
  (44 other events, 516.6 us)
Sparse Core Ops, SparseCore 0:
  10.4 26.7 all-gather.6
  130.8 32.8 reduce-scatter.5
  288.7 24.0 all-gather.14
  326.6 33.0 reduce-scatter.9
Sparse Core Ops, SparseCore 1:
  134.0 41.2 all-gather.10
  177.3 22.4 all-gather.8
  202.6 41.5 all-gather.12
  249.7 31.5 reduce-scatter.7
  366.5 23.9 all-gather.16
  393.5 19.3 reduce-scatter.13
  430.1 235.4 all-reduce.4
  668.1 32.1 reduce-scatter.11
where the time goes:
time: 773 us; the launch traced here: 764 us
  waiting for transfers between devices  366 us (47%)
  blocking collectives  204 us (26%)
  matrix products  78.5 us (10%)
  other arithmetic  50.3 us (7%)
  local copies, waits for them, and re-layouts  41.4 us (5%)
  between operations  22.8 us (3%)
    psum x1, waiting for transfers between devices, body(): lax.psum((grad_qkv, grad_out, grad_up, grad_down, table_sum, column_grad)...  184 us
    psum x1, blocking collectives, body(): total_squares = lax.psum(squares, ('dp', 'mp'))  39.3 us
    psum x1, blocking collectives, body(): lax.psum((grad_qkv, grad_out, grad_up, grad_down, table_sum, column_grad)...  39.3 us
    all_gather x1, blocking collectives, body(): lax.all_gather(lowered[0], 'dp', axis=1, tiled=True)  35.4 us
    reduce_scatter x1, waiting for transfers between devices, body(): lax.psum_scatter(normed_part.astype(jnp.bfloat16), 'mp', scatter_dimensio...  33.2 us
    all_gather x1, blocking collectives, body(): lax.all_gather(lowered[1], 'dp', axis=1, tiled=True)  31 us
    reduce_scatter x1, waiting for transfers between devices, body(): lax.psum_scatter(second_part.astype(jnp.bfloat16), 'mp', scatter_dimensio...  30.7 us
    all_gather x1, blocking collectives, body(): lax.all_gather(lowered[4], 'dp', axis=2, tiled=True)  30.6 us
  transfers between devices with their start and end apart: 12, of which 9 were waited for; matrix products, arithmetic and copies ran while one was open for 12% of the time, Pallas kernels for 0%

commit v1 on v0

v1 whole, which is shorter than its diff:
```python
import functools
import jax
import jax.numpy as jnp
import numpy as np
from jax import lax
from jax.sharding import Mesh, PartitionSpec as P
from jax.experimental import pallas as pl
from jax.experimental.pallas import tpu as pltpu

MESH = pl.DeviceIdType.MESH
F32 = jnp.float32
BF16 = jnp.bfloat16
HD = 64
STEP = 5

norm_epsilon = 1e-06
adam_epsilon = 1e-08
learn_rates = (0.02, 0.1, 0.02, 0.02, 0.5, 0.5)
beta_first = 0.5
beta_second = 0.5
decay_rate = 0.01
clip_limit = 0.05
mask_fill = -1000000000.0
score_scale = 0.125

ATT, UP, DOWN = 0, 1, 2


def pick(index, values):
    out = values[-1]
    for k in range(len(values) - 1):
        out = jnp.where(index == k, values[k], out)
    return out


class Place:
    def __init__(self):
        outer = lax.axis_index("outer")
        self.sub = lax.axis_index("inner")
        self.m = lax.axis_index("mp")
        self.z = outer // 2
        self.x = lax.rem(outer, 2)
        self.y = self.m // 2
        self.c = lax.rem(self.m, 2)
        self.first = self.c == 0
        self.sib = self.at(c=1 - self.c)
        x, y = self.line(1, 0)
        self.second = self.at(x=x, y=y)
        x, y = self.line(0, 1)
        self.third = self.at(x=x, y=y)

    def at(self, z=None, x=None, y=None, c=None):
        z = self.z if z is None else z
        x = self.x if x is None else x
        y = self.y if y is None else y
        c = self.c if c is None else c
        return (z * 2 + x, self.sub, y * 2 + c)

    def mate(self, m):
        return (self.z * 2 + self.x, self.sub, m)

    def line(self, side, far, other_core=False):
        first = (1 - self.c if other_core else self.c) == 0
        x = jnp.where(first, side, far)
        y = jnp.where(first, far, side)
        return self.x + x - 2 * self.x * x, self.y + y - 2 * self.y * y

    def order(self, t):
        return pick(self.z, [(0, 1, 2, 3), (1, 0, 3, 2), (2, 2, 1, 1), (3, 3, 0, 0)][t])


def remote(src, dst, send, recv, device):
    return pltpu.make_async_remote_copy(
        src_ref=src, dst_ref=dst, send_sem=send, recv_sem=recv, device_id=device, device_id_type=MESH
    )


def greet(place, mids):
    barrier = pltpu.get_barrier_semaphore()

    def hello(device):
        pl.semaphore_signal(barrier, inc=1, device_id=device, device_id_type=MESH)

    z = place.z
    hello(place.sib)
    hello(place.second)
    hello(place.third)
    hello(place.at(z=z + 2 - 4 * (z // 2)))
    pl.when(z > 0)(lambda: hello(place.at(z=z - 1)))
    pl.when(z < 3)(lambda: hello(place.at(z=z + 1)))
    count = 4 + jnp.where(z > 0, 1, 0) + jnp.where(z < 3, 1, 0)
    if mids:
        inside = (place.m == 1) | (place.m == 2)
        pl.when(inside)(lambda: hello((place.z * 2 + place.x, place.sub, 3 - place.m)))
        count = count + jnp.where(inside, 1, 0)
    pl.semaphore_wait(barrier, count)


class Gather:
    def __init__(self, place, g, chunks, sems):
        self.p, self.g, self.chunks = place, g, chunks
        self.sems = sems
        self.width = g.shape[4] // 4
        self.sent = []

    def piece(self, j, z, side, far, core=False):
        x, y = self.p.line(side, far, core)
        c = 1 - self.p.c if core else self.p.c
        a, low, w = self.chunks[j]
        cols = pl.ds(pl.multiple_of((y * 2 + c) * self.width + low, 128), w)
        if z is None:
            return self.g.at[a, :, x, :, cols]
        return self.g.at[a, z, x, :, cols]

    def go(self, ref, send, recv, device, when=None):
        copy = remote(ref, ref, send, recv, device)
        if when is None:
            copy.start()
        else:
            pl.when(when)(copy.start)
        self.sent.append((copy, when))

    def arrived(self, ref, recv):
        remote(ref, ref, recv, recv, self.p.sib).wait_recv()

    def z_send(self, a, src, index, to, when):
        zs, zr = self.sems[0], self.sems[1]
        self.go(self.piece(a, src, 0, 0), zs.at[a, index], zr.at[a, src], self.p.at(z=to), when)

    def side_sends(self, a, src):
        zs, zr, ps, pr, ts, tr, cs, cr = self.sems
        self.go(self.piece(a, src, 0, 0), ts.at[a, src], tr.at[a, src], self.p.third)
        self.go(self.piece(a, src, 0, 0), ps.at[a, src], pr.at[a, src], self.p.second)

    def core_send(self, a, k, side, far):
        cs, cr = self.sems[6], self.sems[7]
        self.go(self.piece(a, None, side, far), cs.at[a, k], cr.at[a, k], self.p.sib)

    def own(self, a):
        z = self.p.z
        self.z_send(a, z, z, z + 1, z < 3)
        self.z_send(a, z, 4, z - 1, z > 0)
        self.side_sends(a, z)

    def z_step(self, a, t):
        z = self.p.z
        src = self.p.order(t)
        self.arrived(self.piece(a, src, 0, 0), self.sems[1].at[a, src])
        to = jnp.where(z > src, z + 1, z - 1)
        self.z_send(a, src, src, to, (to >= 0) & (to <= 3))
        self.side_sends(a, src)
        if t == 3:
            self.core_send(a, 0, 0, 0)

    def p_step(self, a, t):
        src = self.p.order(t)
        ts, tr = self.sems[4], self.sems[5]
        self.arrived(self.piece(a, src, 1, 0), self.sems[3].at[a, src])
        self.go(self.piece(a, src, 1, 0), ts.at[a, 4 + src], tr.at[a, 4 + src], self.p.third)
        if t == 3:
            self.core_send(a, 1, 1, 0)

    def t_step(self, a, side):
        for t in range(4):
            src = self.p.order(t)
            self.arrived(self.piece(a, src, side, 1), self.sems[5].at[a, side * 4 + src])
        self.core_send(a, 2 + side, side, 1)

    def front(self, a):
        for t in range(4):
            if t:
                self.z_step(a, t)
            if t:
                self.p_step(a, t - 1)
        self.p_step(a, 3)

    def core_wait(self, a):
        for k, (side, far) in enumerate(((0, 0), (1, 0), (0, 1), (1, 1))):
            self.arrived(self.piece(a, None, side, far, True), self.sems[7].at[a, k])

    def finish(self):
        for copy, when in self.sent:
            if when is None:
                copy.wait_send()
            else:
                pl.when(when)(copy.wait_send)


def gather_sems(chunks):
    sizes = (5, 4, 4, 4, 8, 8, 4, 4)
    return [pltpu.SemaphoreType.DMA((chunks, n)) for n in sizes]


def overlaps(rows, length):
    pairs = []
    for m in range(3):
        edge = (m + 1) * rows
        low = edge // length * length
        if low == edge:
            continue
        pairs.append((m, m + 1, max(low, m * rows), edge))
        pairs.append((m + 1, m, edge, min(low + length, edge + rows)))
    return pairs


class Share:
    def __init__(self, place, pairs, src, dst, sems):
        self.p, self.pairs, self.src, self.dst, self.sems = place, pairs, src, dst, sems

    def copy(self, pair):
        source, target, low, high = pair
        k = 0 if source < target else 1
        return remote(self.src(low, high, target), self.dst(low, high, target), self.sems.at[k], self.sems.at[2 + k], self.p.mate(target))

    def start(self):
        for pair in self.pairs:
            pl.when(self.p.m == pair[0])(self.copy(pair).start)

    def wait_recv(self):
        for pair in self.pairs:
            pl.when(self.p.m == pair[1])(self.copy(pair).wait_recv)

    def wait_send(self):
        for pair in self.pairs:
            pl.when(self.p.m == pair[0])(self.copy(pair).wait_send)


class Sum5:
    def __init__(self, place, table, slots, sems):
        self.p, self.table, self.slots, self.sems = place, table, slots, sems
        z = place.z
        self.peers = [
            place.at(z=z + 1 - 2 * lax.rem(z, 2)),
            place.at(z=z + 2 - 4 * (z // 2)),
            place.at(x=1 - place.x),
            place.at(y=1 - place.y),
            place.sib,
        ]

    def copy(self, k):
        return remote(self.slots.at[5 + k], self.slots.at[k], self.sems.at[k], self.sems.at[5 + k], self.peers[k])

    def start(self, k):
        self.slots[5 + k] = self.table[...]
        self.copy(k).start()

    def end(self, k):
        self.copy(k).wait_recv()
        self.table[...] = self.table[...] + self.slots[k]

    def finish(self):
        for k in range(5):
            self.copy(k).wait_send()


class Scatter:
    def __init__(self, place, g, chunks, rc, r3, r2, ru, rd, sems, emit):
        self.p, self.g, self.chunks = place, g, chunks
        self.rc, self.r3, self.r2, self.ru, self.rd = rc, r3, r2, ru, rd
        self.sems = sems
        self.emit = emit
        self.width = g.shape[4] // 4
        self.sent = []

    def cols(self, j, y, c):
        a, low, w = self.chunks[j]
        return pl.ds(pl.multiple_of((y * 2 + c) * self.width + low, 128), w)

    def region(self, j, side, far, core=False):
        x, y = self.p.line(side, far, core)
        c = 1 - self.p.c if core else self.p.c
        return (self.chunks[j][0], slice(None), x, slice(None), self.cols(j, y, c))

    def go(self, src, dst, send, recv, device, when=None):
        copy = remote(src, dst, send, recv, device)
        if when is None:
            copy.start()
        else:
            pl.when(when)(copy.start)
        self.sent.append((copy, when))

    def arrived(self, ref, recv):
        remote(ref, ref, recv, recv, self.p.sib).wait_recv()

    def core_start(self, j):
        cs, cr = self.sems[0], self.sems[1]
        for far in (1, 0):
            for side in (1, 0):
                k = far * 2 + side
                self.go(
                    self.g.at[self.region(j, side, far, True)], self.rc.at[j, k], cs.at[j, k], cr.at[j, k], self.p.sib
                )

    def add(self, j, side, far, other):
        a, z, x, r, cols = self.region(j, side, far)

        def step(k):
            here = self.g[a, k, x, :, cols].astype(F32)
            self.g[a, k, x, :, cols] = (here + other(k).astype(F32)).astype(BF16)

        pl.loop(0, 4)(step)

    def core_end(self, j):
        ts, tr = self.sems[2], self.sems[3]
        for far in (1, 0):
            for side in (1, 0):
                k = far * 2 + side
                self.arrived(self.rc.at[j, k], self.sems[1].at[j, k])
                self.add(j, side, far, lambda q, k=k: self.rc[j, k, q])
                if far == 1:
                    self.go(
                        self.g.at[self.region(j, side, 1)], self.r3.at[j, side], ts.at[j, side], tr.at[j, side], self.p.third
                    )

    def third_end(self, j):
        ps, pr = self.sems[4], self.sems[5]
        for side in (1, 0):
            self.arrived(self.r3.at[j, side], self.sems[3].at[j, side])
            self.add(j, side, 0, lambda q, side=side: self.r3[j, side, q])
            if side == 1:
                self.go(self.g.at[self.region(j, 1, 0)], self.r2.at[j], ps.at[j], pr.at[j], self.p.second)

    def line_ref(self, j, z):
        a, _, x, r, cols = self.region(j, 0, 0)
        return self.g.at[a, z, x, r, cols]

    def up(self, j, d, when):
        us, ur = self.sems[6], self.sems[7]
        self.go(self.line_ref(j, d), self.ru.at[j, d], us.at[j, d], ur.at[j, d], self.p.at(z=self.p.z + 1), when)

    def down(self, j, d, when):
        ds, dr = self.sems[8], self.sems[9]
        self.go(self.line_ref(j, d), self.rd.at[j, d], ds.at[j, d], dr.at[j, d], self.p.at(z=self.p.z - 1), when)

    def second_end(self, j):
        z = self.p.z
        self.arrived(self.r2.at[j], self.sems[5].at[j])
        self.add(j, 0, 0, lambda q: self.r2[j, q])
        for d in range(3):
            self.up(j, 3 - d, z == 0)
            self.down(j, d, z == 3)

    def relay(self, j, d, buf, recv, when, send):
        def run():
            self.arrived(buf.at[j, d], recv.at[j, d])
            ref = self.line_ref(j, d)
            ref[...] = (ref[...].astype(F32) + buf[j, d].astype(F32)).astype(BF16)

        pl.when(when)(run)
        send(j, d, when)

    def z_step(self, j, t):
        z = self.p.z
        up, down = 3 - t, t
        if up >= 2:
            self.relay(j, up, self.ru, self.sems[7], (z > 0) & (z < up), self.up)
        if down <= 1:
            self.relay(j, down, self.rd, self.sems[9], (z < 3) & (z > down), self.down)

    def last(self, j):
        z = self.p.z
        a, low, w = self.chunks[j]
        x, y = self.p.x, self.p.y
        total = self.g[a, z, x, :, self.cols(j, y, self.p.c)].astype(F32)
        self.emit(j, total, True)

        def from_below():
            self.arrived(self.ru.at[j, z], self.sems[7].at[j, z])
            self.emit(j, self.ru[j, z].astype(F32), False)

        def from_above():
            self.arrived(self.rd.at[j, z], self.sems[9].at[j, z])
            self.emit(j, self.rd[j, z].astype(F32), False)

        pl.when(z > 0)(from_below)
        pl.when(z < 3)(from_above)

    def finish(self):
        for copy, when in self.sent:
            if when is None:
                copy.wait_send()
            else:
                pl.when(when)(copy.wait_send)


def scatter_scratch(chunks, rows):
    n = len(chunks)
    w = chunks[0][2]
    return [
        pltpu.VMEM((n, 4, 4, rows, w), BF16),
        pltpu.VMEM((n, 2, 4, rows, w), BF16),
        pltpu.VMEM((n, 4, rows, w), BF16),
        pltpu.VMEM((n, 4, rows, w), BF16),
        pltpu.VMEM((n, 4, rows, w), BF16),
    ], [
        pltpu.SemaphoreType.DMA(s)
        for s in ((n, 4), (n, 4), (n, 2), (n, 2), (n,), (n,), (n, 4), (n, 4), (n, 4), (n, 4))
    ]


def pipeline(stages, count):
    for step in range(count + len(stages) - 1):
        for s in range(len(stages)):
            j = step - s
            if 0 <= j < count:
                stages[s](j)


def nt(a, b):
    return lax.dot_general(a, b, (((1,), (1,)), ((), ())), preferred_element_type=F32)


def tn(a, b):
    return lax.dot_general(a, b, (((0,), (0,)), ((), ())), preferred_element_type=F32)


def nn(a, b):
    return jnp.dot(a, b, preferred_element_type=F32)


def even_lanes(shape):
    return lax.broadcasted_iota(jnp.int32, shape, 1) < HD


def keep(values, even):
    mask = even_lanes(values.shape)
    zero = jnp.zeros_like(values)
    return jnp.where(mask, values, zero) if even else jnp.where(mask, zero, values)


def col_sum(values):
    return jnp.sum(values, 0, keepdims=True)


class Layer:
    def __init__(self, refs, place):
        self.__dict__.update(refs)
        self.p = place
        self.rows, self.width = self.tok.shape
        self.length = self.seg.shape[1]
        self.blocks = self.rows // 128
        self.cols = self.g.shape[4] // 4
        self.hidden = self.g.shape[4]
        self.s0 = self.rows * place.m // self.length
        self.s1 = (self.rows * place.m + self.rows - 1) // self.length
        self.window = self.kv.shape[1]

    def w(self, a, low, size):
        return self.g[a, :, :, :, pl.ds(pl.multiple_of(low, 128), size)].reshape(self.width, size)

    def put(self, a, low, value):
        size = value.shape[1]
        shape = self.g.shape[1:4] + (size,)
        self.g[a, :, :, :, pl.ds(pl.multiple_of(low, 128), size)] = value.astype(BF16).reshape(shape)

    def gain(self, row):
        return self.tab[pl.ds(row, 1), :]

    def blk(self, i):
        return pl.ds(pl.multiple_of(i * 128, 128), 128)

    def seq_of(self, i):
        return (self.rows * self.p.m + 128 * i) // self.length

    def each_seq(self, run):
        for s in range(self.window):
            if s == 0:
                run(s)
            else:
                pl.when(self.s0 + s <= self.s1)(functools.partial(run, s))

    def masks(self):
        n = self.length
        for i in range(self.blocks):
            s = self.seq_of(i)
            at = lax.rem(self.rows * self.p.m + 128 * i, n)
            seg = self.seg[pl.ds(s, 1), :]
            grp = self.grp[pl.ds(s, 1), :]
            ans = self.ans[pl.ds(s, 1), :]
            seg_q = pick(at // 128, [seg[:, k : k + 128] for k in range(0, n, 128)])
            grp_q = pick(at // 128, [grp[:, k : k + 128] for k in range(0, n, 128)])
            code = jnp.where(seg_q == 0, -1, grp_q).astype(F32)
            code = jnp.transpose(jnp.broadcast_to(code, (8, 128)))[:, :1]
            open_key = (seg == 0) | (ans == 1)
            rule = (code == grp.astype(F32)) | (code < 0.0) | open_key
            position = lax.broadcasted_iota(jnp.int32, (1, n), 1)
            seen = rule & (position < self.pad[s])
            self.bias[i] = jnp.where(seen, 0.0, mask_fill)

    def project(self):
        c = self.cols

        @pl.loop(0, 4)
        def _(b):
            row = self.tab[pl.ds(6 + b, 1), :]
            lanes = lax.broadcasted_iota(jnp.int32, (1, 256), 1) < c // 4
            q = nn(self.tok[...], self.w(ATT, b * c, 256)) + row[:, :256]
            self.q[b] = jnp.where(lanes, q * score_scale, 0.0).astype(BF16)
            wkv = self.w(ATT, b * c + c // 2, c // 2)

            def one(s):
                kv = nn(self.tokw[s], wkv) + row[:, c // 2 :]
                self.kv[b, s] = kv.astype(BF16)

            self.each_seq(one)

    def heads(self, b, i):
        s = self.seq_of(i) - self.s0
        q0 = self.q[b, self.blk(i), :128]
        q2 = self.q[b, self.blk(i), 128:]
        return s, keep(q0, True), keep(q0, False), q2

    def attend(self):
        @pl.loop(0, 4 * self.blocks)
        def _(k):
            b, i = k // self.blocks, lax.rem(k, self.blocks)
            s, q0, q1, q2 = self.heads(b, i)
            bias = self.bias[i]

            def softmax(scores):
                scores = scores + bias
                e = jnp.exp(scores - jnp.max(scores, -1, keepdims=True))
                return (e * (1.0 / jnp.sum(e, -1, keepdims=True))).astype(BF16)

            t0, t1, t2 = (self.kv[b, s, :, 128 * t : 128 * t + 128] for t in range(3))
            s01 = nt(jnp.concatenate([q0, q1], 0), t0)
            p0, p1, p2 = softmax(s01[:128]), softmax(s01[128:]), softmax(nt(q2, t1))
            self.shares[b, i, 0] = p0
            self.shares[b, i, 1] = p1
            self.shares[b, i, 2] = p2
            o12 = nn(jnp.concatenate([p1, p2], 0), t2)
            self.o[b, self.blk(i), :128] = keep(nn(p0, t1), False).astype(BF16)
            self.o[b, self.blk(i), 128:] = jnp.where(even_lanes((128, 128)), o12[:128], o12[128:]).astype(BF16)

    def row_loop(self, step, sums):
        n = 48

        def run(k, carry):
            at = pl.ds(pl.multiple_of(k * n, n), n)
            return step(at, carry)

        zero = tuple(jnp.zeros((1, self.width), F32) for _ in range(sums))
        return lax.fori_loop(0, self.rows // n, run, zero)

    def first_norm(self):
        self.acc[...] = jnp.zeros_like(self.acc)

        @pl.loop(0, 4)
        def _(b):
            self.acc[...] += nt(self.o[b], self.w(ATT, b * self.cols + 128, 256))

        g1, b1, co = self.gain(0), self.gain(1), self.gain(2)

        def step(at, carry):
            r = self.tok[at, :].astype(F32) + (self.acc[at, :] + co)
            r = r - jnp.mean(r, -1, keepdims=True)
            rs = lax.rsqrt(jnp.mean(r * r, -1, keepdims=True) + norm_epsilon)
            xh = r * rs
            self.xh[at, :] = xh
            self.rs[at, :] = rs
            self.hb[at, :] = (xh * g1 + b1).astype(BF16)
            return carry

        self.row_loop(step, 0)

    def up(self):
        n = 256

        def part(b, k):
            low = pl.multiple_of(b * self.cols + k, n)
            u = nn(self.hb[...], self.w(UP, low, n)) + self.tab[pl.ds(10 + b, 1), k : k + n]
            share = 0.5 + 0.5 * lax.erf(u * np.float32(np.sqrt(0.5)))
            slope = share + u * (jnp.exp(-0.5 * (u * u)) * np.float32(1 / np.sqrt(2 * np.pi)))
            self.act[:, pl.ds(low, n)] = (u * share).astype(BF16)
            self.slope[:, pl.ds(low, n)] = slope.astype(BF16)

        self.hidden_loop(part, n)

    def hidden_loop(self, part, n):
        @pl.loop(0, 4)
        def _(b):
            for k in range(0, self.cols, n):
                part(b, k)

    def long_nt(self, left, a):
        n = 512

        @pl.loop(0, self.hidden // n)
        def _(j):
            low = pl.multiple_of(j * n, n)
            self.acc[...] += nt(left[:, pl.ds(low, n)], self.w(a, low, n))

    def second_norm(self):
        self.acc[...] = jnp.zeros_like(self.acc)
        self.long_nt(self.act, DOWN)
        g1, b1, g2, b2, cd = self.gain(0), self.gain(1), self.gain(3), self.gain(4), self.gain(5)

        def step(at, carry):
            r = (self.xh[at, :] * g1 + b1) + (self.acc[at, :] + cd)
            r = r - jnp.mean(r, -1, keepdims=True)
            rs = lax.rsqrt(jnp.mean(r * r, -1, keepdims=True) + norm_epsilon)
            xh = r * rs
            self.block_out[at, :] = (xh * g2 + b2).astype(BF16)
            grad = self.out_grad[at, :].astype(F32)
            inner = grad * g2
            back = rs * (inner - jnp.mean(inner, -1, keepdims=True) - xh * jnp.mean(inner * xh, -1, keepdims=True))
            self.acc[at, :] = back
            low = back.astype(BF16)
            self.dz[at, :] = low
            return carry[0] + col_sum(grad * xh), carry[1] + col_sum(grad), carry[2] + col_sum(low.astype(F32))

        dg, db, dc = self.row_loop(step, 3)
        self.sums[3:4, :] = dg
        self.sums[4:5, :] = db
        self.sums[5:6, :] = dc

    def hidden_back(self):
        n = 256

        def part(b, k):
            low = pl.multiple_of(b * self.cols + k, n)
            at = pl.ds(low, n)
            du = (nn(self.dz[...], self.w(DOWN, low, n)) * self.slope[:, at].astype(F32)).astype(BF16)
            self.slope[:, at] = du
            self.sums[pl.ds(10 + b, 1), k : k + n] = col_sum(du.astype(F32))

        self.hidden_loop(part, n)

    def weight_grad(self, a, left, right):
        n = 256
        self.turned[...] = left[...].T

        @pl.loop(0, self.hidden // n)
        def _(j):
            low = pl.multiple_of(j * n, n)
            self.put(a, low, nn(self.turned[...], right[:, pl.ds(low, n)]))

    def first_back(self):
        self.long_nt(self.slope, UP)
        g1 = self.gain(0)

        def step(at, carry):
            grad = self.acc[at, :]
            xh = self.xh[at, :]
            inner = grad * g1
            back = self.rs[at, :] * (
                inner - jnp.mean(inner, -1, keepdims=True) - xh * jnp.mean(inner * xh, -1, keepdims=True)
            )
            self.acc[at, :] = back
            low = back.astype(BF16)
            self.dz[at, :] = low
            return carry[0] + col_sum(grad * xh), carry[1] + col_sum(grad), carry[2] + col_sum(low.astype(F32))

        dg, db, dc = self.row_loop(step, 3)
        self.sums[0:1, :] = dg
        self.sums[1:2, :] = db
        self.sums[2:3, :] = dc

    def attend_back(self):
        c = self.cols

        @pl.loop(0, 4)
        def _(b):
            do = nn(self.dz[...], self.w(ATT, b * c + 128, 256))
            lanes = lax.broadcasted_iota(jnp.int32, (1, 256), 1) >= HD
            self.do[...] = jnp.where(lanes, do, 0.0).astype(BF16)
            self.dkv_acc[...] = jnp.zeros_like(self.dkv_acc)

            @pl.loop(0, self.blocks)
            def _(i):
                s, q0, q1, q2 = self.heads(b, i)
                t0, t1, t2 = (self.kv[b, s, :, 128 * t : 128 * t + 128] for t in range(3))
                do0 = self.do[self.blk(i), :128]
                do12 = self.do[self.blk(i), 128:]
                do1, do2 = keep(do12, True), keep(do12, False)
                dp12 = nt(jnp.concatenate([do1, do2], 0), t2)

                def back(h, dp):
                    low = self.shares[b, i, h]
                    p = low.astype(F32)
                    scaled = p * dp
                    return low, (scaled - p * jnp.sum(scaled, -1, keepdims=True)).astype(BF16)

                p0, ds0 = back(0, nt(do0, t1))
                p1, ds1 = back(1, dp12[:128])
                p2, ds2 = back(2, dp12[128:])
                dq01 = nn(jnp.concatenate([ds0, ds1], 0), t0)
                dq0 = jnp.where(even_lanes((128, 128)), dq01[:128], dq01[128:])
                dq2 = keep(nn(ds2, t1), True)
                self.q[b, self.blk(i), :128] = (dq0 * score_scale).astype(BF16)
                self.q[b, self.blk(i), 128:] = (dq2 * score_scale).astype(BF16)
                rows = jnp.concatenate
                self.dkv_acc[s, :, :128] += tn(rows([ds0, ds1], 0), rows([q0, q1], 0))
                self.dkv_acc[s, :, 128:256] += tn(rows([ds2, p0], 0), rows([q2, do0], 0))
                self.dkv_acc[s, :, 256:] += tn(rows([p1, p2], 0), rows([do1, do2], 0))

            total = jnp.zeros((1, c // 2), F32)
            for s in range(self.window):
                low = self.dkv_acc[s].astype(BF16)
                self.kv[b, s] = low
                total = total + col_sum(low.astype(F32))
            first = col_sum(self.q[b].astype(F32))
            gap = jnp.zeros((1, c // 2 - 256), F32)
            self.sums[pl.ds(6 + b, 1), :] = jnp.concatenate([first, gap, total], 1)

    def input_back(self):
        c, half = self.cols, self.width // 2

        @pl.loop(0, 4)
        def _(b):
            self.acc[...] += nt(self.q[b], self.w(ATT, b * c, 256))

        def one(s):
            self.dkv_acc[...] = jnp.zeros_like(self.dkv_acc)

            @pl.loop(0, 4)
            def _(b):
                w = self.w(ATT, b * c + c // 2, c // 2)
                for k in range(2):
                    self.dkv_acc[k] += nt(self.kv[b, s], w[k * half : k * half + half])

            for k in range(2):
                self.xw[s, :, k * half : k * half + half] = self.dkv_acc[k].astype(BF16)

        self.each_seq(one)

    def attention_grads(self):
        c = self.cols
        self.turned[...] = self.tok[...].T
        self.turned2[...] = self.dz[...].T

        def turn(s):
            self.turnedw[s] = self.tokw[s].T

        self.each_seq(turn)

        @pl.loop(0, 4)
        def _(b):
            dq = nn(self.turned[...], self.q[b])
            do = nn(self.turned2[...], self.o[b])
            self.put(ATT, b * c, dq[:, :128])
            self.put(ATT, b * c + 128, dq[:, 128:] + do[:, :128])
            self.put(ATT, b * c + 256, do[:, 128:])

            def finish(count):
                total = nn(self.turnedw[0], self.kv[b, 0])
                for s in range(1, count):
                    total = total + nn(self.turnedw[s], self.kv[b, s])
                self.put(ATT, b * c + c // 2, total)

            for count in range(1, self.window + 1):
                pl.when(self.s1 - self.s0 + 1 == count)(functools.partial(finish, count))


CHUNKS = 2


def gather_chunks(cols):
    w = cols // CHUNKS
    return [(a, k * w, w) for a in (ATT, UP, DOWN) for k in range(CHUNKS)]


def scatter_chunks(cols):
    w = cols // CHUNKS
    return [(a, k * w, w) for a in (DOWN, UP, ATT) for k in range(CHUNKS)]


INPUTS = ("shard", "small", "tok", "out_grad", "seg", "grp", "ans", "pad")
OUTPUTS = ("block_out", "input_grad", "owned", "total")


def kernel(names, chunks, back_chunks, pairs, *refs):
    r = dict(zip(names, refs))
    pc = Place()
    gather = Gather(pc, r["g"], chunks, [r["gs%d" % k] for k in range(8)])
    r["table"][...] = r["small"][...]
    for j, (a, low, w) in enumerate(chunks):
        ref = gather.piece(j, pc.z, 0, 0)
        ref[...] = r["shard"][a, :, low : low + w]
    layer = Layer(r, pc)
    rows = layer.rows
    greet(pc, True)
    tok, tokw = r["tok"], r["tokw"]

    share = Share(
        pc,
        pairs,
        lambda low, high, target: tok.at[pl.ds(low % rows, high - low)],
        lambda low, high, target: tokw.at[in_window(low, high, target, rows, layer.length)],
        r["share_sems"],
    )
    spread = Sum5(pc, r["table"], r["table_slots"], r["table_sems"])
    spread.start(0)
    share.start()
    for m in range(4):

        def own_tokens(m=m):
            for at, where in own_parts(m, rows, layer.length):
                tokw[where[0], where[1], :] = tok[at, :]

        pl.when(pc.m == m)(own_tokens)
    layer.masks()
    n = len(chunks)
    gather.own(0)
    gather.own(1)
    for j in range(n + 1):
        if j < n:
            gather.front(j)
            if j + 2 < n:
                gather.own(j + 2)
        if j < 5:
            spread.end(j)
            if j < 4:
                spread.start(j + 1)
        if j >= 1:
            gather.t_step(j - 1, 0)
            gather.t_step(j - 1, 1)
        if j >= 2:
            gather.core_wait(j - 2)
    gather.core_wait(n - 1)
    share.wait_recv()
    gather.finish()
    share.wait_send()
    spread.finish()

    r["tab"][...] = r["table"][...].astype(F32)
    layer.project()
    layer.attend()
    layer.first_norm()
    layer.up()
    layer.second_norm()
    layer.hidden_back()
    layer.weight_grad(DOWN, r["dz"], r["act"])
    layer.first_back()
    layer.weight_grad(UP, r["hb"], r["slope"])
    layer.attend_back()
    layer.input_back()

    window = r["xw"]

    xr = r["xrecv"]
    homes = [(t, s, low, high) for s, t, low, high in pairs]

    def home_copy(pair):
        k = 0 if pair[0] < pair[1] else 1
        size = pair[3] - pair[2]
        return remote(
            window.at[in_window(pair[2], pair[3], pair[0], rows, layer.length)],
            xr.at[k, pl.ds(0, size)],
            r["home_sems"].at[k],
            r["home_sems"].at[2 + k],
            pc.mate(pair[1]),
        )

    for pair in homes:
        pl.when(pc.m == pair[0])(home_copy(pair).start)
    layer.attention_grads()

    owned = r["owned"]

    def emit(j, value, first):
        a, low, w = back_chunks[j]
        if first:
            owned[a, :, low : low + w] = value
        else:
            owned[a, :, low : low + w] += value

    sc = Scatter(pc, r["g"], back_chunks, r["rc"], r["r3"], r["r2"], r["ru"], r["rd"], [r["ss%d" % k] for k in range(10)], emit)
    pipeline(
        [sc.core_start, sc.core_end, sc.third_end, sc.second_end, lambda j: sc.z_step(j, 0), lambda j: sc.z_step(j, 1), sc.last],
        len(back_chunks),
    )

    for m in range(4):

        def own_rows(m=m):
            for at, where in own_parts(m, rows, layer.length):
                r["acc"][at, :] += window[where[0], where[1], :].astype(F32)

        pl.when(pc.m == m)(own_rows)
    for pair in homes:

        def take(pair=pair):
            home_copy(pair).wait_recv()
            k = 0 if pair[0] < pair[1] else 1
            low, high = pair[2] - pair[1] * rows, pair[3] - pair[1] * rows
            r["acc"][low:high, :] += xr[k, : high - low, :].astype(F32)

        pl.when(pc.m == pair[1])(take)
    r["input_grad"][...] = r["acc"][...].astype(BF16)

    sums = r["sums"]
    squares = jnp.zeros((1, owned.shape[2]), F32)
    for a in range(3):
        squares = squares + col_sum(owned[a] * owned[a])
    sums[14:15, :] = squares
    sums[15:16, :] = jnp.zeros_like(squares)
    total = Sum5(pc, sums, r["sum_slots"], r["sum_sems"])
    for k in range(5):
        total.start(k)
        total.end(k)
    r["total"][...] = sums[...]
    for pair in homes:
        pl.when(pc.m == pair[0])(home_copy(pair).wait_send)
    sc.finish()
    total.finish()


def in_window(low, high, m, rows, length):
    return low // length - m * rows // length, pl.ds(low % length, high - low)


def own_parts(m, rows, length):
    parts, low = [], m * rows
    while low < (m + 1) * rows:
        high = min((m + 1) * rows, (low // length + 1) * length)
        parts.append((slice(low - m * rows, high - m * rows), in_window(low, high, m, rows, length)))
        low = high
    return parts


def run_layer(shard, small, tok, out_grad, seg, grp, ans, pad):
    _, per, cols = shard.shape
    rows, width = tok.shape
    length = seg.shape[1]
    hidden = 4 * cols
    window = max((m * rows + rows - 1) // length - m * rows // length + 1 for m in range(4))
    blocks = rows // 128
    pairs = overlaps(rows, length)
    chunks, back_chunks = gather_chunks(cols), scatter_chunks(cols)
    most = max(high - low for _, _, low, high in pairs)
    bufs, sems = scatter_scratch(back_chunks, per)
    scratch = {
        "g": pltpu.VMEM((3, 4, 2, per, hidden), BF16),
        "table": pltpu.VMEM((16, width), BF16),
        "tab": pltpu.VMEM((16, width), F32),
        "table_slots": pltpu.VMEM((10, 16, width), BF16),
        "tokw": pltpu.VMEM((window, length, width), BF16),
        "bias": pltpu.VMEM((blocks, 128, length), F32),
        "q": pltpu.VMEM((4, rows, 256), BF16),
        "kv": pltpu.VMEM((4, window, length, cols // 2), BF16),
        "shares": pltpu.VMEM((4, blocks, 3, 128, length), BF16),
        "o": pltpu.VMEM((4, rows, 256), BF16),
        "do": pltpu.VMEM((rows, 256), BF16),
        "dkv_acc": pltpu.VMEM((window, length, cols // 2), F32),
        "acc": pltpu.VMEM((rows, width), F32),
        "xh": pltpu.VMEM((rows, width), F32),
        "rs": pltpu.VMEM((rows, 1), F32),
        "hb": pltpu.VMEM((rows, width), BF16),
        "dz": pltpu.VMEM((rows, width), BF16),
        "act": pltpu.VMEM((rows, hidden), BF16),
        "slope": pltpu.VMEM((rows, hidden), BF16),
        "turned": pltpu.VMEM((width, rows), BF16),
        "turned2": pltpu.VMEM((width, rows), BF16),
        "turnedw": pltpu.VMEM((window, width, length), BF16),
        "xw": pltpu.VMEM((window, length, width), BF16),
        "xrecv": pltpu.VMEM((2, most, width), BF16),
        "sums": pltpu.VMEM((16, width), F32),
        "sum_slots": pltpu.VMEM((10, 16, width), F32),
        "share_sems": pltpu.SemaphoreType.DMA((4,)),
        "home_sems": pltpu.SemaphoreType.DMA((4,)),
        "table_sems": pltpu.SemaphoreType.DMA((10,)),
        "sum_sems": pltpu.SemaphoreType.DMA((10,)),
    }
    scratch.update(zip(("rc", "r3", "r2", "ru", "rd"), bufs))
    scratch.update(("gs%d" % k, s) for k, s in enumerate(gather_sems(len(chunks))))
    scratch.update(("ss%d" % k, s) for k, s in enumerate(sems))
    names = INPUTS + OUTPUTS + tuple(scratch)
    vmem = pl.BlockSpec(memory_space=pltpu.VMEM)
    return pl.pallas_call(
        functools.partial(kernel, names, chunks, back_chunks, pairs),
        out_shape=[
            jax.ShapeDtypeStruct((rows, width), BF16),
            jax.ShapeDtypeStruct((rows, width), BF16),
            jax.ShapeDtypeStruct((3, per, cols), F32),
            jax.ShapeDtypeStruct((16, width), F32),
        ],
        in_specs=[vmem] * 7 + [pl.BlockSpec(memory_space=pltpu.SMEM)],
        out_specs=[vmem] * 4,
        scratch_shapes=list(scratch.values()),
        compiler_params=pltpu.CompilerParams(collective_id=0, has_side_effects=True, vmem_limit_bytes=62 * 2**20),
        name="layer",
    )(shard, small, tok, out_grad, seg, grp, ans, pad)


def adam_update(weight, grad, first, second, factor, decayed, rate):
    clipped = grad * factor
    first_new = beta_first * first + (1.0 - beta_first) * clipped
    second_new = beta_second * second + (1.0 - beta_second) * clipped * clipped
    ratio = (
        first_new
        / (1.0 - beta_first**STEP)
        / (jnp.sqrt(second_new / (1.0 - beta_second**STEP)) + adam_epsilon)
    )
    if decayed:
        ratio = ratio + decay_rate * weight
    return (weight - rate * ratio, first_new, second_new)


def body(tokens, out_grad, segment_ids, group_ids, answer_ids, pad_lengths, *states):
    masters, firsts, seconds = states[:6], states[6:12], states[12:]
    qkv, out, up, down, norm, bias = [m.astype(BF16) for m in masters]
    inner = lax.axis_size("inner")
    place = lax.axis_index("outer") * inner + lax.axis_index("inner")
    mp = lax.axis_index("mp")
    width = tokens.shape[1]
    local = qkv.shape[2]
    attention = jnp.concatenate([qkv[0], out.T, qkv[1], qkv[2]], 1)
    shard = jnp.stack([attention, up, down.T])
    part = norm.shape[2]
    norm_rows = lax.dynamic_update_slice(jnp.zeros((6, width), BF16), norm[:, 0], (0, mp * local + place * part))
    columns = bias.shape[1] * inner * lax.axis_size("outer")
    line = lax.dynamic_update_slice(jnp.zeros((columns,), BF16), bias[0], (place * bias.shape[1],))
    line_att = jnp.concatenate([line[:local], jnp.zeros((2 * local,), BF16), line[local : 2 * local]])
    spread = jnp.arange(4)[:, None] == mp
    zero = jnp.zeros((), BF16)
    small = jnp.concatenate(
        [norm_rows, jnp.where(spread, line_att, zero), jnp.where(spread, line[2 * local :], zero), jnp.zeros((2, width), BF16)]
    )
    if inner > 1:
        shard = lax.all_gather(shard, "inner", axis=1, tiled=True)
        small = lax.psum(small, "inner")
    block_out, input_grad, owned, total = run_layer(
        shard, small, tokens, out_grad, segment_ids, group_ids, answer_ids, pad_lengths
    )
    squares = total[14]
    if inner > 1:
        owned = lax.psum_scatter(owned, "inner", scatter_dimension=1, tiled=True)
        total = lax.psum(total, "inner")
        squares = lax.psum(jnp.sum(owned * owned), ("outer", "inner", "mp"))
    small_rows = total[:14]
    table_sum = small_rows[:6]
    query_sum = small_rows[6:10, :local]
    value_sum = small_rows[6:10, 3 * local :]
    up_sum = small_rows[10:14]
    small_squares = sum(jnp.sum(v * v) for v in (table_sum, query_sum, value_sum, up_sum))
    grad_norm = jnp.sqrt(jnp.sum(squares) + small_squares)
    factor = jnp.minimum(1.0, clip_limit / grad_norm)
    line = jnp.concatenate([query_sum, value_sum, up_sum], 1)
    grads = [
        jnp.stack([owned[0, :, :local], owned[0, :, 2 * local : 3 * local], owned[0, :, 3 * local :]]),
        owned[0, :, local : 2 * local].T,
        owned[1],
        owned[2].T,
        lax.dynamic_slice(table_sum, (0, mp * local + place * part), (6, part))[:, None],
        lax.dynamic_slice(line, (mp, place * bias.shape[1]), (1, bias.shape[1])),
    ]
    updated = [
        adam_update(masters[k], grads[k], firsts[k], seconds[k], factor, k < 4, learn_rates[k]) for k in range(6)
    ]
    return (block_out, input_grad, grad_norm) + tuple(updated[k][part] for part in range(3) for k in range(6))


def solution(mesh):
    dp = mesh.shape["dp"]
    outer = 8
    grid = Mesh(mesh.devices.reshape(outer, dp // outer, mesh.shape["mp"]), ("outer", "inner", "mp"))
    d = ("outer", "inner")
    both = P(d + ("mp",), None)
    states = (P(None, d, "mp"), P("mp", d), P(d, "mp"), P("mp", d), P(None, "mp", d), P("mp", d))
    in_specs = (both, both, P(d, None), P(d, None), P(d, None), P(d)) + states * 3
    out_specs = (both, both, P()) + states * 3
    return jax.shard_map(body, mesh=grid, in_specs=in_specs, out_specs=out_specs, check_vma=False)
```

time: 773 us -> 285 us (0.37)
  waiting for transfers between devices: 366 us -> 0 us
  Pallas kernels: 0 us -> 250 us
  blocking collectives: 204 us -> 0 us
  matrix products: 78.5 us -> 0 us
  other arithmetic: 50.3 us -> 12 us
  local copies, waits for them, and re-layouts: 41.4 us -> 14.4 us
  between operations: 22.8 us -> 5.33 us
    pallas_call x0 -> x1, Pallas kernels: none -> 250 us  [run_layer(): pl.pallas_call(functools.partial(kernel, names, chunks, back_chunks, pair...]
    psum x1 -> x0, waiting for transfers between devices: 184 us -> none  [body(): lax.psum((grad_qkv, grad_out, grad_up, grad_down, table_sum, column_grad)...]
    all_gather x4 -> x0, blocking collectives: 102 us -> none  [the longest x1 35.4 us: body(): lax.all_gather(lowered[0], 'dp', axis=1, tiled=True)]
    all_gather x6 -> x0, waiting for transfers between devices: 92.7 us -> none  [the longest x1 29.2 us: body(): lax.all_gather(lowered[3], 'dp', axis=1, tiled=True)]
    reduce_scatter x5 -> x0, waiting for transfers between devices: 87.9 us -> none  [the longest x1 33.2 us: body(): lax.psum_scatter(normed_part.astype(jnp.bfloat16), 'mp', scatter_dimensio...]
    psum x2 -> x0, blocking collectives: 78.7 us -> none  [the longest x1 39.3 us: body(): total_squares = lax.psum(squares, ('dp', 'mp'))]
    dot_general x32 -> x0, matrix products: 75.3 us -> none  [the longest x1 15.2 us: body(): jnp.dot(normed_full, up_weight, preferred_element_type=jnp.float32)]
    unnamed x1 -> x0, blocking collectives: 23.1 us -> none
  transfers between devices with their start and end apart: 12 -> 0, of which waited for: 9 -> 0; matrix products, arithmetic and copies ran while one was open for 12% -> 0% of each run, Pallas kernels for 0% -> 0%
where the time goes in v1:
time: 285 us; the launch traced here: 282 us
  Pallas kernels  250 us (88%)
  local copies, waits for them, and re-layouts  14.4 us (5%)
  other arithmetic  12 us (4%)
  between operations  5.33 us (2%)
    pallas_call x1, Pallas kernels, run_layer(): pl.pallas_call(functools.partial(kernel, names, chunks, back_chunks, pair...  250 us
    unnamed x56, local copies, waits for them, and re-layouts  13.6 us

profile of v1, /device:TPU:0, one launch (start us, length us, event | category | flops | bytes accessed | tf_op | source)
XLA Modules:
  0.0 281.8 jit_solution(12036722900244390279)
XLA Ops:
  0.7 0.7 copy-done.19
  1.9 0.7 copy-done.16
  2.8 0.7 maximum_maximum_fusion.refs_1_
  3.5 1.0 convert_element_type.18
  4.5 0.9 copy-done.12
  5.6 0.8 copy-done
  6.4 0.9 copy-done.1
  7.4 0.8 pad_maximum_fusion.refs_0_
  8.2 250.1 %layer.1 = (bf16[384,768]{1,0:T(8,128)(2,1)}, bf16[384,768]{1,0:T(8,128)(2,1)}, f32[3,96,768]{2,1,0:T(8,128)}, f32[16,768]{1,0:T(8,128)}) custom-call(bf16[3,96,768]{2,1,0:T(8,128)(2,1)} %pad_maximum_fusion.refs_0_, bf16[16,768]{1,0:T(8,128)(2,1)} %maximum_maximum_fusion.refs_1_, bf16[384,768]{1,0:T(8,128)(2,1)} %refs_2_.1, bf16[384,768]{1,0:T(8,128)(2,1)} %refs_3_.1, ...), custom_call_target="tpu_custom_call" | custom-call | tf_op jit(solution)/shard_map/layer/pallas_call | solution.py:970
  258.3 1.5 multiply_reduce_fusion.2
  259.8 1.3 fusion.17
  265.8 0.7 copy-done.20
  266.5 0.7 multiply_subtract_fusion.4
  267.1 0.7 copy-done.18
  269.7 2.1 multiply_subtract_fusion
  271.9 1.1 multiply_subtract_fusion.1
  273.0 0.8 copy-done.14
  274.1 0.7 copy.54
  274.8 0.7 copy.56
  275.6 0.7 copy.58
  276.4 0.9 copy-done.2
  277.4 1.1 multiply_subtract_fusion.2
  278.6 0.8 copy.77
  279.8 0.8 copy.78
  (66 shorter events, 5.3 us)
Async XLA Ops:
  0.7 0.7 copy-start.19
  1.9 0.7 copy-start.16
  4.5 0.9 copy-start.12
  5.5 1.0 copy-start
  6.4 1.0 copy-start.1
  8.2 261.5 %copy-start.6 = (f32[768,96]{0,1:T(8,128)S(1)}, f32[768,96]{0,1:T(8,128)}, u32[]{:S(2)}) copy-start(f32[768,96]{0,1:T(8,128)} %param.39) | copy-start | bytes 884740
  8.2 261.5 %copy-start.7 = (f32[768,96]{0,1:T(8,128)S(1)}, f32[768,96]{0,1:T(8,128)}, u32[]{:S(2)}) copy-start(f32[768,96]{0,1:T(8,128)} %param.45) | copy-start | bytes 884740
  258.3 2.9 %copy-start.15 = (f32[16,768]{1,0:T(8,128)S(1)}, f32[16,768]{1,0:T(8,128)}, u32[]{:S(2)}) copy-start(f32[16,768]{1,0:T(8,128)} %get-tuple-element.27) | copy-start | bytes 147460
  265.8 0.7 copy-start.20
  265.8 0.7 copy-start.21
  267.1 0.7 copy-start.18
  267.1 0.7 copy-start.17
  269.7 2.2 copy-start.3
  269.7 2.2 copy-start.8
  269.7 2.2 copy-start.9
  271.9 1.1 copy-start.13
  272.9 0.9 copy-start.14
  274.8 1.6 copy-start.11
  276.3 1.0 copy-start.2
  276.3 1.0 copy-start.10
  277.4 1.2 copy-start.5
  278.6 1.3 copy-start.4
